TPU v7x, 32 devices: a whole 2x2x4 slice. The times are simulated.
32 devices in a mesh: dp: 4 (over y, x), space: 8 (over z, core).
Axes of the slice: x: 2, y: 2, z: 4, core: 2. Of those that a mesh axis runs over, the one named last changes fastest.
Arguments:
- volume: bfloat16 [4, 32, 16, 16, 128], P('dp', None, 'space'), may hold values from -6 to 6
- kernel: bfloat16 [64, 32, 3, 3, 3], replicated, may hold values from -0.21875 to 0.21875
- cotangent: bfloat16 [4, 64, 8, 8, 64], P('dp', None, 'space'), may hold values from -6 to 6
Outputs:
- activated: bfloat16 [4, 64, 8, 8, 64], P('dp', None, 'space')
- grad_volume: bfloat16 [4, 32, 16, 16, 128], P('dp', None, 'space')
- grad_kernel: float32 [64, 32, 3, 3, 3], replicated
All inputs are finite; a program needn't handle non-finite values.
Results may differ from a plain program's by a relative error of at most 0.0049.
Values may be sent and summed in bfloat16 or wider, within the bound.
A program may use at most 64 MiB of HBM per device.

v0:
```python
import jax
import jax.numpy as jnp
from jax import lax
from jax.sharding import PartitionSpec as P


def from_behind(block, axis, distance):
    devices = range(lax.axis_size(axis))
    route = [(i - distance, i) for i in devices if i - distance in devices]
    return lax.ppermute(block, axis, route)


def convolve(inputs, weights, low, high):
    return lax.conv_general_dilated(
        inputs,
        weights,
        (2, 2, 2),
        [(low, high), (1, 1), (1, 1)],
        dimension_numbers=("NCDHW", "OIDHW", "NCDHW"),
        preferred_element_type=jnp.float32,
    )


def input_grad(grads, weights, low, high):
    flipped = weights[:, :, ::-1, ::-1, ::-1]
    return lax.conv_general_dilated(
        grads,
        flipped,
        (1, 1, 1),
        [(low, high), (1, 2), (1, 2)],
        lhs_dilation=(2, 2, 2),
        dimension_numbers=("NCDHW", "IODHW", "NCDHW"),
        preferred_element_type=jnp.float32,
    )


def weight_grad(inputs, grads):
    return lax.conv_general_dilated(
        inputs,
        grads,
        (1, 1, 1),
        [(0, 0), (1, 0), (1, 0)],
        rhs_dilation=(2, 2, 2),
        dimension_numbers=("CNDHW", "IODHW", "CNDHW"),
        preferred_element_type=jnp.float32,
    )


def per_device(volume, kernel, cotangent):
    below = from_behind(volume[:, :, -1:], "space", 1)
    extended = jnp.concatenate([below, volume], axis=2)
    pre = convolve(extended, kernel, 0, 0)
    activated = (0.01 * pre + 0.99 * jax.nn.softplus(pre)).astype(jnp.bfloat16)
    local_grad = (cotangent.astype(jnp.float32) * (0.01 + 0.99 * jax.nn.sigmoid(pre))).astype(
        jnp.bfloat16
    )
    grad_extended = input_grad(local_grad, kernel, 2, 2)
    kernel_local = weight_grad(extended, local_grad)
    grad_input = grad_extended[:, :, 1:]
    next_grad = from_behind(local_grad[:, :, :1], "space", -1)
    from_above = input_grad(next_grad, kernel, 2, 0)
    grad_input = grad_input.at[:, :, -1:].add(from_above)
    kernel_total = lax.psum(kernel_local, ("dp", "space"))
    total_cells = (
        volume.shape[0]
        * lax.axis_size("dp")
        * volume.shape[2]
        * lax.axis_size("space")
        * volume.shape[3]
        * volume.shape[4]
        / 8.0
    )
    grad_kernel = kernel_total / jnp.sqrt(jnp.float32(total_cells))
    return (activated, grad_input.astype(jnp.bfloat16), grad_kernel)


def solution(mesh):
    placed = (P("dp", None, "space", None, None), P(), P("dp", None, "space", None, None))
    return jax.shard_map(
        per_device,
        mesh=mesh,
        in_specs=placed,
        out_specs=(P("dp", None, "space", None, None), P("dp", None, "space", None, None), P()),
        check_vma=False,
    )
```

profile of v0, /device:TPU:0, one launch (start us, length us, event | category | flops | bytes accessed | tf_op | source)
XLA Modules:
  0.0 173.6 jit_solution(3309809939613104812)
XLA Ops:
  7.2 0.0 copy-start
  7.2 0.0 all-reduce.2.cloned.1.call-start
  7.2 1.0 slice.40
  8.2 2.4 %collective-permute-start = (bf16[1,32,1,16,128]{4,3,2,1,0:T(8,128)(2,1)S(1)}, bf16[1,32,1,16,128]{4,3,2,1,0:T(8,128)(2,1)S(1)}, u32[]{:S(2)}, u32[]{:S(2)}) collective-permute-start(bf16[1,32,1,16,128]{4,3,2,1,0:T(8,128)(2,1)S(1)} %slice.40), channel_id=1, source_target_pairs={{0,1},{1,2},{2,3},{3,4},{4,5},{5,6},{6,7},{8,9},{9,10},{10,11},{11... | collective-permute-start | bytes 393224 | tf_op jit(solution)/shard_map/ppermute | solution.py:10
  10.6 1.1 copy.32
  11.6 0.0 collective-permute-done
  11.7 1.0 constant_dynamic-update-slice_fusion
  12.7 3.6 %copy.41 = bf16[1,32,3,16,128]{1,0,4,3,2:T(2,128)(2,1)} copy(bf16[1,32,3,16,128]{4,3,2,1,0:T(8,128)(2,1)S(1)} %constant_dynamic-update-slice_fusion) | data formatting | bytes 786432 | tf_op jit(solution)/shard_map/concatenate | solution.py:51
  16.3 1.2 copy.45
  17.4 0.3 pad.2.clone
  17.8 0.0 copy-start.3
  17.8 0.7 copy.30
  18.5 0.1 slice.51
  18.5 0.0 copy-done
  18.5 0.0 copy-done.3
  18.5 1.3 multiply_add_fusion
  19.8 0.0 copy-start.2
  19.9 0.1 copy.33
  20.0 1.5 collective-permute-start.1
  21.6 0.0 copy-done.2
  21.6 1.2 convolution_select_fusion
  22.8 0.0 copy-start.1
  22.8 0.8 copy.36
  23.5 1.2 slice_bitcast_fusion
  24.7 0.0 copy-done.1
  24.7 7.1 %fusion.18 = f32[64,32,3,3,3]{0,1,4,3,2:T(8,128)} fusion(bf16[1,32,3,16,128]{1,0,4,3,2:T(2,128)(2,1)S(1)} %copy-done.1, bf16[1,64,1,8,64]{1,3,4,0,2:T(8,128)(2,1)S(1)} %fusion.17), kind=kOutput, calls=%fused_computation.24 | convolution fusion | flops 53981184 | bytes 679936 | tf_op jit(solution)/shard_map/conv_general_dilated | solution.py:38
  31.8 0.8 copy.43
  32.6 0.0 all-reduce.2.cloned.1.call-update
  32.6 0.0 collective-permute-done.1
  32.7 0.8 fusion.5
  33.6 0.2 copy.39
  33.7 0.8 fusion.9
  34.6 2.9 %copy.44 = bf16[1,32,2,16,128]{4,3,2,1,0:T(8,128)(2,1)} copy(bf16[1,32,2,16,128]{1,3,4,2,0:T(8,128)(2,1)} %fusion.9) | data formatting | bytes 524288
  37.5 127.4 %all-reduce.2.cloned.1.call-done = f32[64,32,3,3,3]{0,1,4,3,2:T(8,128)} async-done(((f32[64,32,3,3,3]{0,1,4,3,2:T(8,128)}), f32[64,32,3,3,3]{0,1,4,3,2:T(8,128)}) %all-reduce.2.cloned.1.call-update) | async-done | bytes 221200 | tf_op jit(solution)/shard_map/psum | solution.py:63
  164.9 1.8 %broadcast_multiply_fusion = f32[64,32,3,3,3]{0,1,4,3,2:T(8,128)} fusion(f32[64,32,3,3,3]{0,1,4,3,2:T(8,128)} %all-reduce.2.cloned.1.call-done), kind=kLoop, calls=%fused_computation.26 | loop fusion | flops 55296 | bytes 442368 | tf_op jit(solution)/shard_map/div | solution.py:73
  (10 shorter events, 0.2 us)
Async XLA Ops:
  7.2 11.4 %copy-start = (bf16[64,32,3,3,3]{0,1,4,3,2:T(8,128)(2,1)S(1)}, bf16[64,32,3,3,3]{0,1,4,3,2:T(8,128)(2,1)}, u32[]{:S(2)}) copy-start(bf16[64,32,3,3,3]{0,1,4,3,2:T(8,128)(2,1)} %param.6) | copy-start | bytes 331780
  7.2 157.7 %all-reduce.2.cloned.1.call-start = ((), (), s32[]{:S(2)}) async-start(), calls=%async_computation | async-start | bytes 884736 | tf_op jit(solution)/shard_map/psum | solution.py:63
  8.2 3.5 %collective-permute-start = (bf16[1,32,1,16,128]{4,3,2,1,0:T(8,128)(2,1)S(1)}, bf16[1,32,1,16,128]{4,3,2,1,0:T(8,128)(2,1)S(1)}, u32[]{:S(2)}, u32[]{:S(2)}) collective-permute-start(bf16[1,32,1,16,128]{4,3,2,1,0:T(8,128)(2,1)S(1)} %slice.40), channel_id=1, source_target_pairs={{0,1},{1,2},{2,3},{3,4},{4,5},{5,6},{6,7},{8,9},{9,10},{10,11},{11... | collective-permute-start | bytes 393224 | tf_op jit(solution)/shard_map/ppermute | solution.py:10
  17.8 0.8 copy-start.3
  19.8 1.7 copy-start.2
  20.0 12.7 %collective-permute-start.1 = (bf16[1,64,1,8,64]{1,3,4,0,2:T(8,128)(2,1)S(1)}, bf16[1,64,1,8,64]{1,3,4,0,2:T(8,128)(2,1)S(1)}, u32[]{:S(2)}, u32[]{:S(2)}) collective-permute-start(bf16[1,64,1,8,64]{1,3,4,0,2:T(8,128)(2,1)S(1)} %fusion.17), channel_id=1, source_target_pairs={{1,0},{2,1},{3,2},{4,3},{5,4},{6,5},{7,6},{9,8},{10,9},{11,10},{12... | collective-permute-start | bytes 196616 | tf_op jit(solution)/shard_map/ppermute | solution.py:10
  22.8 1.9 %copy-start.1 = (bf16[1,32,3,16,128]{1,0,4,3,2:T(2,128)(2,1)S(1)}, bf16[1,32,3,16,128]{1,0,4,3,2:T(2,128)(2,1)}, u32[]{:S(2)}) copy-start(bf16[1,32,3,16,128]{1,0,4,3,2:T(2,128)(2,1)} %copy.41) | copy-start | bytes 1179652
Sparse Core Ops, SparseCore 0:
  32.8 132.1 all-reduce.1
where the time goes:
time: 174 us
  waiting for transfers between devices  127 us (73%)
  local copies, waits for them, and re-layouts  15.8 us (9%)
  between operations  14.3 us (8%)
  matrix products  10.4 us (6%)
  starting transfers between devices  3.87 us (2%)
  other arithmetic  1.85 us (1%)
    psum x1, waiting for transfers between devices, per_device(): kernel_total = lax.psum(kernel_local, ('dp', 'space'))  127 us
    conv_general_dilated x1, matrix products, weight_grad(): lax.conv_general_dilated(inputs, grads, (1, 1, 1), [(0, 0), (1, 0), (1, 0...  7.09 us
    unnamed x13, local copies, waits for them, and re-layouts  6.03 us
    concatenate x3, local copies, waits for them, and re-layouts, per_device(): extended = jnp.concatenate([below, volume], axis=2)  4.9 us
    ppermute x2, starting transfers between devices, from_behind(): return lax.ppermute(block, axis, route)  3.84 us
  transfers between devices with their start and end apart: 3, of which 1 were waited for; matrix products, arithmetic and copies ran while one was open for 10% of the time, Pallas kernels for 0%

commit v1 on v0

v1 whole, which is shorter than its diff:
```python
import functools
import math

import jax
import jax.numpy as jnp
from jax import lax
from jax.experimental import pallas as pl
from jax.experimental.pallas import tpu as pltpu
from jax.sharding import PartitionSpec as P

F32, BF16 = jnp.float32, jnp.bfloat16
MESH = pl.DeviceIdType.MESH


def dot(a, b, contract):
    return lax.dot_general(a, b, ((contract[0], contract[1]), ((), ())), preferred_element_type=F32)


def picks(rows, cols):
    half, z = rows // 128, rows % 128
    c, half_out, cell = cols // 128, (cols // 64) % 2, cols % 64
    return jnp.where((half == half_out) & (z == 2 * cell + c - 1), 1.0, 0.0).astype(BF16)


def spreads(rows, cols):
    half, cell = rows // 64, rows % 64
    c, half_out, z = cols // 256, (cols // 128) % 2, cols % 128
    return jnp.where((half == half_out) & (z == 2 * cell + c - 1), 1.0, 0.0).astype(BF16)


def kernel(nd, ns, root, v_ref, k_ref, c_ref, act_ref, gv_ref, gk_ref,
           halo, vf, vh, left, x_s, cf, gsend, gnext, gz, gout, term,
           recv_a, part, recv_b, gath, full,
           halo_sem, g_sem, send_a, sem_a, send_b, sem_b, send_c, sem_c, send_d, sem_d):
    d, s = lax.axis_index("dp"), lax.axis_index("space")
    ci, co = v_ref.shape[0], c_ref.shape[0]
    sub = term.shape[0] // (nd * ns)
    chunk = sub * ns

    barrier = pltpu.get_barrier_semaphore()
    for k in range(1, nd):
        pl.semaphore_signal(barrier, inc=1, device_id=(lax.rem(d + k, nd), s), device_id_type=MESH)
    for k in range(1, ns):
        pl.semaphore_signal(barrier, inc=1, device_id=(d, lax.rem(s + k, ns)), device_id_type=MESH)

    vf[...] = v_ref[...].astype(F32).reshape(vf.shape)
    pick = picks(lax.broadcasted_iota(jnp.int32, (256, 384), 0), lax.broadcasted_iota(jnp.int32, (256, 384), 1))
    spread = spreads(lax.broadcasted_iota(jnp.int32, (128, 768), 0), lax.broadcasted_iota(jnp.int32, (128, 768), 1))

    pl.semaphore_wait(barrier, nd + ns - 2)

    def up(src, dst):
        return pltpu.make_async_remote_copy(src_ref=src, dst_ref=dst, send_sem=halo_sem.at[0], recv_sem=halo_sem.at[1],
                                            device_id=(d, lax.rem(s + 1, ns)), device_id_type=MESH)

    def down(src, dst):
        return pltpu.make_async_remote_copy(src_ref=src, dst_ref=dst, send_sem=g_sem.at[0], recv_sem=g_sem.at[1],
                                            device_id=(d, lax.rem(s + ns - 1, ns)), device_id_type=MESH)

    @pl.when(s < ns - 1)
    def _():
        up(v_ref.at[:, 1], halo).start()

    def gather_plane(a, ref, first, stride):
        planes = [ref[pl.ds(first + y, ci, stride=stride), :].astype(BF16) for y in range(16)]
        for b in range(3):
            for cell in range(8):
                y, row = 2 * cell + b - 1, ((a * 3 + b) * 4 + cell // 2) * ci
                block = planes[y] if y >= 0 else jnp.zeros((ci, 128), BF16)
                left[row:row + ci, (cell % 2) * 128:(cell % 2) * 128 + 128] = block
        rows = 12 * ci
        picked = dot(left[a * rows:(a + 1) * rows, :], pick, ((1,), (0,))).astype(BF16)
        for b in range(3):
            for j in range(4):
                for c in range(3):
                    row = ((a * 3 + b) * 3 + c) * ci
                    x_s[row:row + ci, j * 128:j * 128 + 128] = picked[(b * 4 + j) * ci:(b * 4 + j + 1) * ci, c * 128:c * 128 + 128]

    gather_plane(1, vf, 0, 32)
    gather_plane(2, vf, 16, 32)
    third = 9 * ci
    pre = dot(k_ref[third:, :], x_s[third:, :], ((0,), (0,)))
    cf[:, :64] = c_ref[...].astype(F32).reshape(co * 8, 64)
    cot = jnp.concatenate(
        [cf[pl.ds(y, co, stride=8), :][:, :64] for y in range(8)], axis=1)

    @pl.when(s > 0)
    def _():
        up(v_ref.at[:, 1], halo).wait_recv()
        vh[...] = halo[...].astype(F32).reshape(vh.shape)

    @pl.when(s == 0)
    def _():
        vh[...] = jnp.zeros_like(vh)

    gather_plane(0, vh, 0, 16)
    pre = pre + dot(k_ref[:third, :], x_s[:third, :], ((0,), (0,)))
    e = jnp.exp(-jnp.abs(pre))
    inverse = 1.0 / (1.0 + e)
    sigmoid = jnp.where(pre >= 0, inverse, e * inverse)
    grad = (cot * (0.01 + 0.99 * sigmoid)).astype(BF16)
    gsend[...] = grad

    @pl.when(s > 0)
    def _():
        down(gsend, gnext).start()

    rows = 27 * ci // 2
    none = jnp.zeros_like(grad)
    term[:rows, :] = dot(x_s[:rows, :], jnp.concatenate([grad, none], axis=0), ((1,), (1,))) + dot(
        x_s[rows:, :], jnp.concatenate([none, grad], axis=0), ((1,), (1,)))
    term[rows:, :] = jnp.zeros((term.shape[0] - rows, 128), F32)

    def copy_a(k):
        to = lax.rem(d + k, nd)
        return pltpu.make_async_remote_copy(
            src_ref=term.at[pl.ds(pl.multiple_of(to * chunk, chunk), chunk)], dst_ref=recv_a.at[k - 1],
            send_sem=send_a.at[k - 1], recv_sem=sem_a.at[k - 1], device_id=(to, s), device_id_type=MESH)

    def copy_b(k):
        to = lax.rem(s + k, ns)
        return pltpu.make_async_remote_copy(
            src_ref=part.at[pl.ds(pl.multiple_of(to * sub, sub), sub)], dst_ref=recv_b.at[k - 1],
            send_sem=send_b.at[k - 1], recv_sem=sem_b.at[k - 1], device_id=(d, to), device_id_type=MESH)

    def copy_c(k):
        return pltpu.make_async_remote_copy(
            src_ref=gath.at[pl.ds(pl.multiple_of(s * sub, sub), sub)],
            dst_ref=gath.at[pl.ds(pl.multiple_of(s * sub, sub), sub)],
            send_sem=send_c.at[k - 1], recv_sem=sem_c.at[k - 1],
            device_id=(d, lax.rem(s + k, ns)), device_id_type=MESH)

    def copy_d(k):
        return pltpu.make_async_remote_copy(
            src_ref=gath, dst_ref=full.at[pl.ds(pl.multiple_of(d * chunk, chunk), chunk)],
            send_sem=send_d.at[k - 1], recv_sem=sem_d.at[k - 1],
            device_id=(lax.rem(d + k, nd), s), device_id_type=MESH)

    for k in range(1, nd):
        copy_a(k).start()

    softplus = jnp.maximum(pre, 0.0) + jnp.log1p(e)
    act = 0.01 * pre + 0.99 * softplus
    for j in range(4):
        pair = act[:, j * 128:j * 128 + 128]
        cf[pl.ds(2 * j, co, stride=8), :] = pair
        cf[pl.ds(2 * j + 1, co, stride=8), :] = pltpu.roll(pair, 64, 1)
    act_ref[...] = cf[:, :64].reshape(act_ref.shape).astype(BF16)

    def grad_rows(a_list, g):
        stacked = jnp.concatenate([g[:, j * 128:j * 128 + 128] for j in range(4)], axis=0)
        wide = dot(stacked, spread, ((1,), (0,))).astype(BF16)
        for c in range(3):
            for j in range(4):
                gz[c * co:(c + 1) * co, j * 256:j * 256 + 256] = wide[j * co:(j + 1) * co, c * 256:c * 256 + 256]
        total = None
        for c in range(3):
            weights = jnp.concatenate(
                [k_ref[((a * 3 + b) * 3 + c) * ci:((a * 3 + b) * 3 + c + 1) * ci, :] for a in a_list for b in range(3)], axis=0)
            one = dot(weights, gz[c * co:(c + 1) * co, :], ((1,), (0,)))
            total = one if total is None else total + one
        return total

    def tile(total, which, y):
        m = y // 2

        def at(b, cell):
            row = (which * 3 + b) * ci
            return total[row:row + ci, cell * 128:cell * 128 + 128]

        if y % 2 == 0:
            return at(1, m)
        return at(2, m) + at(0, m + 1) if m < 7 else at(2, m)

    own = grad_rows((1, 2), grad)
    for p in range(2):
        for y in range(16):
            gout[pl.ds(p * 16 + y, ci, stride=32), :] = tile(own, p, y)

    for k in range(1, nd):
        copy_a(k).wait_recv()
    total = term[pl.ds(pl.multiple_of(d * chunk, chunk), chunk), :]
    for k in range(1, nd):
        total = total + recv_a[k - 1]
    part[...] = total
    for k in range(1, ns):
        copy_b(k).start()

    @pl.when(s < ns - 1)
    def _():
        down(gsend, gnext).wait_recv()
        above = grad_rows((0,), gnext[...])
        for y in range(16):
            where = pl.ds(16 + y, ci, stride=32)
            gout[where, :] = gout[where, :] + tile(above, 0, y)

    gv_ref[...] = gout[...].astype(BF16).reshape(gv_ref.shape)

    for k in range(1, ns):
        copy_b(k).wait_recv()
    total = part[pl.ds(pl.multiple_of(s * sub, sub), sub), :]
    for k in range(1, ns):
        total = total + recv_b[k - 1]
    gath[pl.ds(pl.multiple_of(s * sub, sub), sub), :] = (total / root).astype(gath.dtype)
    for k in range(1, ns):
        copy_c(k).start()
    for k in range(1, ns):
        copy_c(k).wait_recv()
    for k in range(1, nd):
        copy_d(k).start()
    full[pl.ds(pl.multiple_of(d * chunk, chunk), chunk), :] = gath[...]
    for k in range(1, nd):
        copy_d(k).wait_recv()
    packed = full[:rows, :].astype(F32)
    gk_ref[:rows, :] = packed[:, :64]
    gk_ref[rows:, :] = packed[:, 64:]

    @pl.when(s < ns - 1)
    def _():
        up(v_ref.at[:, 1], halo).wait_send()

    @pl.when(s > 0)
    def _():
        down(gsend, gnext).wait_send()

    for k in range(1, nd):
        copy_a(k).wait_send()
        copy_d(k).wait_send()
    for k in range(1, ns):
        copy_b(k).wait_send()
        copy_c(k).wait_send()


def per_device(volume, weights, cotangent):
    nd, ns = lax.axis_size("dp"), lax.axis_size("space")
    _, ci, planes, gy, gz_ = volume.shape
    co = weights.shape[0]
    cells = volume.shape[0] * nd * planes * ns * gy * gz_ / 8.0
    sub = 16 * max(1, -(-(27 * ci // 2) // (16 * nd * ns)))
    chunk, rows = sub * ns, sub * ns * nd
    dma = pltpu.SemaphoreType.DMA
    vmem = pl.BlockSpec(memory_space=pltpu.VMEM)
    k2 = weights.transpose(2, 3, 4, 1, 0).reshape(27 * ci, co)
    act, gv, gk = pl.pallas_call(
        functools.partial(kernel, nd, ns, math.sqrt(cells)),
        out_shape=(
            jax.ShapeDtypeStruct((co, gy // 2, gz_ // 2), BF16),
            jax.ShapeDtypeStruct((ci, planes, gy, gz_), BF16),
            jax.ShapeDtypeStruct((27 * ci, co), F32),
        ),
        in_specs=[vmem] * 3,
        out_specs=(vmem,) * 3,
        scratch_shapes=[
            pltpu.VMEM((ci, gy, gz_), BF16),
            pltpu.VMEM((ci * 2 * gy, gz_), F32),
            pltpu.VMEM((ci * gy, gz_), F32),
            pltpu.VMEM((36 * ci, 256), BF16),
            pltpu.VMEM((27 * ci, 512), BF16),
            pltpu.VMEM((co * 8, 128), F32),
            pltpu.VMEM((co, 512), BF16),
            pltpu.VMEM((co, 512), BF16),
            pltpu.VMEM((3 * co, 1024), BF16),
            pltpu.VMEM((ci * 2 * gy, gz_), F32),
            pltpu.VMEM((rows, 128), F32),
            pltpu.VMEM((nd - 1, chunk, 128), F32),
            pltpu.VMEM((chunk, 128), F32),
            pltpu.VMEM((ns - 1, sub, 128), F32),
            pltpu.VMEM((chunk, 128), BF16),
            pltpu.VMEM((rows, 128), BF16),
            dma((2,)), dma((2,)),
            dma((nd - 1,)), dma((nd - 1,)), dma((ns - 1,)), dma((ns - 1,)),
            dma((ns - 1,)), dma((ns - 1,)), dma((nd - 1,)), dma((nd - 1,)),
        ],
        compiler_params=pltpu.CompilerParams(collective_id=0, has_side_effects=True, vmem_limit_bytes=44 * 2**20),
        cost_estimate=pl.CostEstimate(flops=400_000_000, bytes_accessed=1_500_000, transcendentals=100_000),
    )(volume[0], k2, cotangent[0, :, 0])
    grad_kernel = gk.reshape(3, 3, 3, ci, co).transpose(4, 3, 0, 1, 2)
    return act[None, :, None], gv[None], grad_kernel


def solution(mesh):
    split = P("dp", None, "space", None, None)
    return jax.shard_map(
        per_device, mesh=mesh, in_specs=(split, P(), split), out_specs=(split, split, P()), check_vma=False)
```

time: 174 us -> 31.1 us (0.18)
  waiting for transfers between devices: 127 us -> 0 us
  Pallas kernels: 0 us -> 25.4 us
  between operations: 14.3 us -> 0.65 us
  local copies, waits for them, and re-layouts: 15.8 us -> 4.9 us
  matrix products: 10.4 us -> 0 us
  starting transfers between devices: 3.87 us -> 0 us
  other arithmetic: 1.85 us -> 0 us
    psum x1 -> x0, waiting for transfers between devices: 127 us -> none  [per_device(): kernel_total = lax.psum(kernel_local, ('dp', 'space'))]
    pallas_call x0 -> x1, Pallas kernels: none -> 25.4 us  [per_device(): pl.pallas_call(functools.partial(kernel, nd, ns, math.sqrt(cells)), out_s...]
    conv_general_dilated x3 -> x0, matrix products: 9.22 us -> none  [the longest x1 7.09 us: weight_grad(): lax.conv_general_dilated(inputs, grads, (1, 1, 1), [(0, 0), (1, 0), (1, 0...]
    concatenate x3 -> x0, local copies, waits for them, and re-layouts: 4.9 us -> none  [per_device(): extended = jnp.concatenate([below, volume], axis=2)]
    ppermute x2 -> x0, starting transfers between devices: 3.84 us -> none  [from_behind(): return lax.ppermute(block, axis, route)]
    slice x5 -> x0, local copies, waits for them, and re-layouts: 2.92 us -> none  [the longest x4 1.96 us: per_device(): grad_input = grad_extended[:, :, 1:]]
    div x1 -> x0, other arithmetic: 1.81 us -> none  [per_device(): grad_kernel = kernel_total / jnp.sqrt(jnp.float32(total_cells))]
    unnamed x13 -> x9, local copies, waits for them, and re-layouts: 6.03 us -> 4.9 us
  transfers between devices with their start and end apart: 3 -> 0, of which waited for: 1 -> 0; matrix products, arithmetic and copies ran while one was open for 10% -> 0% of each run, Pallas kernels for 0% -> 0%
where the time goes in v1:
time: 31.1 us; the launch traced here: 30.9 us
  Pallas kernels  25.4 us (82%)
  local copies, waits for them, and re-layouts  4.9 us (16%)
  between operations  0.65 us (2%)
    pallas_call x1, Pallas kernels, per_device(): pl.pallas_call(functools.partial(kernel, nd, ns, math.sqrt(cells)), out_s...  25.4 us
    unnamed x9, local copies, waits for them, and re-layouts  4.9 us

profile of v1, /device:TPU:0, one launch (start us, length us, event | category | flops | bytes accessed | tf_op | source)
XLA Modules:
  0.0 30.9 jit_solution(13835486168433685805)
XLA Ops:
  0.6 0.0 copy-start
  0.6 0.9 %copy-done = bf16[1,32,2,16,128]{4,3,2,1,0:T(8,128)(2,1)S(1)} copy-done((bf16[1,32,2,16,128]{4,3,2,1,0:T(8,128)(2,1)S(1)}, bf16[1,32,2,16,128]{4,3,2,1,0:T(8,128)(2,1)}, u32[]{:S(2)}) %copy-start) | copy-done | bytes 262168
  1.6 0.0 copy-start.1
  1.6 0.9 %copy-done.1 = bf16[64,32,3,3,3]{0,1,4,3,2:T(8,128)(2,1)S(1)} copy-done((bf16[64,32,3,3,3]{0,1,4,3,2:T(8,128)(2,1)S(1)}, bf16[64,32,3,3,3]{0,1,4,3,2:T(8,128)(2,1)}, u32[]{:S(2)}) %copy-start.1) | copy-done | bytes 110616
  2.5 0.0 copy-start.2
  2.5 0.9 %copy-done.2 = bf16[1,64,1,8,64]{4,3,2,1,0:T(8,128)(2,1)S(1)} copy-done((bf16[1,64,1,8,64]{4,3,2,1,0:T(8,128)(2,1)S(1)}, bf16[1,64,1,8,64]{4,3,2,1,0:T(8,128)(2,1)}, u32[]{:S(2)}) %copy-start.2) | copy-done | bytes 65560
  3.4 25.4 %shard_map.58 = (bf16[64,8,64]{2,1,0:T(8,128)(2,1)S(1)}, bf16[32,2,16,128]{3,2,1,0:T(8,128)(2,1)S(1)}, f32[864,64]{1,0:T(8,128)S(1)}) custom-call(bf16[32,2,16,128]{3,2,1,0:T(8,128)(2,1)S(1)} %bitcast.15, bf16[864,64]{1,0:T(8,128)(2,1)S(1)} %bitcast.16, bf16[64,8,64]{2,1,0:T(8,128)(2,1)S(1)} %bitcast.17), custom_call_target="tpu_custom_call" | custom-call | flops 400000000 | bytes 1500000 | tf_op jit(solution)/shard_map/pallas_call | solution.py:244
  28.8 0.7 %copy.10 = bf16[1,64,1,8,64]{4,3,2,1,0:T(8,128)(2,1)} copy(bf16[1,64,1,8,64]{4,3,2,1,0:T(8,128)(2,1)S(1)} %bitcast.14) | data formatting | bytes 131072
  29.5 0.7 %copy.11 = bf16[1,32,2,16,128]{4,3,2,1,0:T(8,128)(2,1)} copy(bf16[1,32,2,16,128]{4,3,2,1,0:T(8,128)(2,1)S(1)} %bitcast.13) | data formatting | bytes 524288
  30.2 0.8 %copy.12 = f32[64,32,3,3,3]{0,1,4,3,2:T(8,128)} copy(f32[64,32,3,3,3]{0,1,4,3,2:T(8,128)S(1)} %bitcast.12) | data formatting | bytes 442368
Async XLA Ops:
  0.6 1.0 %copy-start = (bf16[1,32,2,16,128]{4,3,2,1,0:T(8,128)(2,1)S(1)}, bf16[1,32,2,16,128]{4,3,2,1,0:T(8,128)(2,1)}, u32[]{:S(2)}) copy-start(bf16[1,32,2,16,128]{4,3,2,1,0:T(8,128)(2,1)} %param.3) | copy-start | bytes 786436
  1.6 0.9 %copy-start.1 = (bf16[64,32,3,3,3]{0,1,4,3,2:T(8,128)(2,1)S(1)}, bf16[64,32,3,3,3]{0,1,4,3,2:T(8,128)(2,1)}, u32[]{:S(2)}) copy-start(bf16[64,32,3,3,3]{0,1,4,3,2:T(8,128)(2,1)} %param.4) | copy-start | bytes 331780
  2.5 0.9 %copy-start.2 = (bf16[1,64,1,8,64]{4,3,2,1,0:T(8,128)(2,1)S(1)}, bf16[1,64,1,8,64]{4,3,2,1,0:T(8,128)(2,1)}, u32[]{:S(2)}) copy-start(bf16[1,64,1,8,64]{4,3,2,1,0:T(8,128)(2,1)} %param.5) | copy-start | bytes 196612

commit v2 on v1

--- a/solution.py
+++ b/solution.py
@@ -28,26 +28,43 @@
     return jnp.where((half == half_out) & (z == 2 * cell + c - 1), 1.0, 0.0).astype(BF16)
 
 
-def kernel(nd, ns, root, v_ref, k_ref, c_ref, act_ref, gv_ref, gk_ref,
-           halo, vf, vh, left, x_s, cf, gsend, gnext, gz, gout, term,
-           recv_a, part, recv_b, gath, full,
-           halo_sem, g_sem, send_a, sem_a, send_b, sem_b, send_c, sem_c, send_d, sem_d):
+def kernel(nd, ns, root, v_hbm, k_hbm, c_hbm, act_hbm, gv_hbm, gk_hbm,
+           v_ref, k_ref, c_ref, in_sem, act_ref, gv_ref, out_sem, halo, vf, vh, left, x_s, cf, gsend, gnext, gz, gout, term,
+           recv_a, part, recv_b, full,
+           halo_sem, g_sem, send_a, sem_a, send_b, sem_b, send_c, sem_c):
     d, s = lax.axis_index("dp"), lax.axis_index("space")
     ci, co = v_ref.shape[0], c_ref.shape[0]
-    sub = term.shape[0] // (nd * ns)
-    chunk = sub * ns
-
+    pair, line = 2, ns // 2
+    group, chunk = nd * pair, term.shape[0] // (nd * pair)
+    core, z = lax.rem(s, pair), s // pair
+    other = lax.rem(s + (ns - 1) - core * (ns - 2), ns)
+
+    def near(k):
+        return lax.rem(d + k // pair, nd), z * pair + lax.rem(core + k % pair, pair)
+
+    def along(k):
+        return d, lax.rem(z + k, line) * pair + core
+
+    def slot(to):
+        return pl.ds(pl.multiple_of((to[0] * pair + lax.rem(to[1], pair)) * chunk, chunk), chunk)
+
+    mine = slot((d, s))
+
+    fetch_v = pltpu.make_async_copy(v_hbm, v_ref, in_sem.at[0])
+    fetch_k = pltpu.make_async_copy(k_hbm, k_ref, in_sem.at[1])
+    fetch_c = pltpu.make_async_copy(c_hbm, c_ref, in_sem.at[2])
+    fetch_v.start()
+    fetch_k.start()
+    fetch_c.start()
     barrier = pltpu.get_barrier_semaphore()
-    for k in range(1, nd):
-        pl.semaphore_signal(barrier, inc=1, device_id=(lax.rem(d + k, nd), s), device_id_type=MESH)
-    for k in range(1, ns):
-        pl.semaphore_signal(barrier, inc=1, device_id=(d, lax.rem(s + k, ns)), device_id_type=MESH)
-
-    vf[...] = v_ref[...].astype(F32).reshape(vf.shape)
+    for to in [near(k) for k in range(1, group)] + [along(k) for k in range(1, line)]:
+        pl.semaphore_signal(barrier, inc=1, device_id=to, device_id_type=MESH)
+    pl.semaphore_signal(barrier, inc=1, device_id=(d, other), device_id_type=MESH)
+
     pick = picks(lax.broadcasted_iota(jnp.int32, (256, 384), 0), lax.broadcasted_iota(jnp.int32, (256, 384), 1))
     spread = spreads(lax.broadcasted_iota(jnp.int32, (128, 768), 0), lax.broadcasted_iota(jnp.int32, (128, 768), 1))
 
-    pl.semaphore_wait(barrier, nd + ns - 2)
+    pl.semaphore_wait(barrier, group + line - 1)
 
     def up(src, dst):
         return pltpu.make_async_remote_copy(src_ref=src, dst_ref=dst, send_sem=halo_sem.at[0], recv_sem=halo_sem.at[1],
@@ -59,7 +76,10 @@
 
     @pl.when(s < ns - 1)
     def _():
-        up(v_ref.at[:, 1], halo).start()
+        up(v_hbm.at[:, 1], halo).start()
+
+    fetch_v.wait()
+    vf[...] = v_ref[...].astype(F32).reshape(vf.shape)
 
     def gather_plane(a, ref, first, stride):
         planes = [ref[pl.ds(first + y, ci, stride=stride), :].astype(BF16) for y in range(16)]
@@ -79,6 +99,8 @@
     gather_plane(1, vf, 0, 32)
     gather_plane(2, vf, 16, 32)
     third = 9 * ci
+    fetch_k.wait()
+    fetch_c.wait()
     pre = dot(k_ref[third:, :], x_s[third:, :], ((0,), (0,)))
     cf[:, :64] = c_ref[...].astype(F32).reshape(co * 8, 64)
     cot = jnp.concatenate(
@@ -86,7 +108,7 @@
 
     @pl.when(s > 0)
     def _():
-        up(v_ref.at[:, 1], halo).wait_recv()
+        up(v_hbm.at[:, 1], halo).wait_recv()
         vh[...] = halo[...].astype(F32).reshape(vh.shape)
 
     @pl.when(s == 0)
@@ -112,40 +134,33 @@
     term[rows:, :] = jnp.zeros((term.shape[0] - rows, 128), F32)
 
     def copy_a(k):
-        to = lax.rem(d + k, nd)
+        to = near(k)
         return pltpu.make_async_remote_copy(
-            src_ref=term.at[pl.ds(pl.multiple_of(to * chunk, chunk), chunk)], dst_ref=recv_a.at[k - 1],
-            send_sem=send_a.at[k - 1], recv_sem=sem_a.at[k - 1], device_id=(to, s), device_id_type=MESH)
+            src_ref=term.at[slot(to)], dst_ref=recv_a.at[k - 1],
+            send_sem=send_a.at[k - 1], recv_sem=sem_a.at[k - 1], device_id=to, device_id_type=MESH)
 
     def copy_b(k):
-        to = lax.rem(s + k, ns)
         return pltpu.make_async_remote_copy(
-            src_ref=part.at[pl.ds(pl.multiple_of(to * sub, sub), sub)], dst_ref=recv_b.at[k - 1],
-            send_sem=send_b.at[k - 1], recv_sem=sem_b.at[k - 1], device_id=(d, to), device_id_type=MESH)
+            src_ref=part, dst_ref=recv_b.at[k - 1],
+            send_sem=send_b.at[k - 1], recv_sem=sem_b.at[k - 1], device_id=along(k), device_id_type=MESH)
 
     def copy_c(k):
         return pltpu.make_async_remote_copy(
-            src_ref=gath.at[pl.ds(pl.multiple_of(s * sub, sub), sub)],
-            dst_ref=gath.at[pl.ds(pl.multiple_of(s * sub, sub), sub)],
-            send_sem=send_c.at[k - 1], recv_sem=sem_c.at[k - 1],
-            device_id=(d, lax.rem(s + k, ns)), device_id_type=MESH)
-
-    def copy_d(k):
-        return pltpu.make_async_remote_copy(
-            src_ref=gath, dst_ref=full.at[pl.ds(pl.multiple_of(d * chunk, chunk), chunk)],
-            send_sem=send_d.at[k - 1], recv_sem=sem_d.at[k - 1],
-            device_id=(lax.rem(d + k, nd), s), device_id_type=MESH)
-
-    for k in range(1, nd):
+            src_ref=full.at[mine], dst_ref=full.at[mine],
+            send_sem=send_c.at[k - 1], recv_sem=sem_c.at[k - 1], device_id=near(k), device_id_type=MESH)
+
+    for k in range(1, group):
         copy_a(k).start()
 
     softplus = jnp.maximum(pre, 0.0) + jnp.log1p(e)
     act = 0.01 * pre + 0.99 * softplus
     for j in range(4):
-        pair = act[:, j * 128:j * 128 + 128]
-        cf[pl.ds(2 * j, co, stride=8), :] = pair
-        cf[pl.ds(2 * j + 1, co, stride=8), :] = pltpu.roll(pair, 64, 1)
+        both = act[:, j * 128:j * 128 + 128]
+        cf[pl.ds(2 * j, co, stride=8), :] = both
+        cf[pl.ds(2 * j + 1, co, stride=8), :] = pltpu.roll(both, 64, 1)
     act_ref[...] = cf[:, :64].reshape(act_ref.shape).astype(BF16)
+    store_act = pltpu.make_async_copy(act_ref, act_hbm, out_sem.at[0])
+    store_act.start()
 
     def grad_rows(a_list, g):
         stacked = jnp.concatenate([g[:, j * 128:j * 128 + 128] for j in range(4)], axis=0)
@@ -177,13 +192,13 @@
         for y in range(16):
             gout[pl.ds(p * 16 + y, ci, stride=32), :] = tile(own, p, y)
 
-    for k in range(1, nd):
+    for k in range(1, group):
         copy_a(k).wait_recv()
-    total = term[pl.ds(pl.multiple_of(d * chunk, chunk), chunk), :]
-    for k in range(1, nd):
+    total = term[mine, :]
+    for k in range(1, group):
         total = total + recv_a[k - 1]
     part[...] = total
-    for k in range(1, ns):
+    for k in range(1, line):
         copy_b(k).start()
 
     @pl.when(s < ns - 1)
@@ -195,40 +210,54 @@
             gout[where, :] = gout[where, :] + tile(above, 0, y)
 
     gv_ref[...] = gout[...].astype(BF16).reshape(gv_ref.shape)
-
-    for k in range(1, ns):
+    store_gv = pltpu.make_async_copy(gv_ref, gv_hbm, out_sem.at[1])
+    store_gv.start()
+
+    for k in range(1, line):
         copy_b(k).wait_recv()
-    total = part[pl.ds(pl.multiple_of(s * sub, sub), sub), :]
-    for k in range(1, ns):
+    total = part[...]
+    for k in range(1, line):
         total = total + recv_b[k - 1]
-    gath[pl.ds(pl.multiple_of(s * sub, sub), sub), :] = (total / root).astype(gath.dtype)
-    for k in range(1, ns):
+    full[mine, :] = (total / root).astype(full.dtype)
+    for k in range(1, group):
         copy_c(k).start()
-    for k in range(1, ns):
+    for k in range(1, group):
         copy_c(k).wait_recv()
-    for k in range(1, nd):
-        copy_d(k).start()
-    full[pl.ds(pl.multiple_of(d * chunk, chunk), chunk), :] = gath[...]
-    for k in range(1, nd):
-        copy_d(k).wait_recv()
-    packed = full[:rows, :].astype(F32)
-    gk_ref[:rows, :] = packed[:, :64]
-    gk_ref[rows:, :] = packed[:, 64:]
-
+    store_gk = pltpu.make_async_copy(full, gk_hbm, out_sem.at[2])
+    store_gk.start()
     @pl.when(s < ns - 1)
     def _():
-        up(v_ref.at[:, 1], halo).wait_send()
+        up(v_hbm.at[:, 1], halo).wait_send()
 
     @pl.when(s > 0)
     def _():
         down(gsend, gnext).wait_send()
 
-    for k in range(1, nd):
+    for k in range(1, group):
         copy_a(k).wait_send()
-        copy_d(k).wait_send()
-    for k in range(1, ns):
+        copy_c(k).wait_send()
+    for k in range(1, line):
         copy_b(k).wait_send()
-        copy_c(k).wait_send()
+    store_act.wait()
+    store_gv.wait()
+    store_gk.wait()
+
+
+def put(act, gv, packed, act_out, gv_out, gk_out, act_v, gv_v, packed_v, gk_v, sem):
+    loads = [pltpu.make_async_copy(x, y, sem.at[i]) for i, (x, y) in enumerate(((packed, packed_v), (gv, gv_v), (act, act_v)))]
+    stores = [pltpu.make_async_copy(x, y, sem.at[i + 3]) for i, (x, y) in enumerate(((gk_v, gk_out), (gv_v, gv_out), (act_v, act_out)))]
+    for load in loads:
+        load.start()
+    loads[0].wait()
+    rows = gk_v.shape[0] // 2
+    gk_v[:rows, :] = packed_v[:rows, :64].astype(F32)
+    gk_v[rows:, :] = packed_v[:rows, 64:].astype(F32)
+    stores[0].start()
+    for load, store in zip(loads[1:], stores[1:]):
+        load.wait()
+        store.start()
+    for store in stores:
+        store.wait()
 
 
 def per_device(volume, weights, cotangent):
@@ -236,21 +265,29 @@
     _, ci, planes, gy, gz_ = volume.shape
     co = weights.shape[0]
     cells = volume.shape[0] * nd * planes * ns * gy * gz_ / 8.0
-    sub = 16 * max(1, -(-(27 * ci // 2) // (16 * nd * ns)))
-    chunk, rows = sub * ns, sub * ns * nd
+    group, line = nd * 2, ns // 2
+    chunk = 16 * max(1, -(-(27 * ci // 2) // (16 * group)))
+    rows = chunk * group
     dma = pltpu.SemaphoreType.DMA
-    vmem = pl.BlockSpec(memory_space=pltpu.VMEM)
+    hbm = pl.BlockSpec(memory_space=pltpu.HBM)
     k2 = weights.transpose(2, 3, 4, 1, 0).reshape(27 * ci, co)
-    act, gv, gk = pl.pallas_call(
+    act, gv, packed = pl.pallas_call(
         functools.partial(kernel, nd, ns, math.sqrt(cells)),
         out_shape=(
             jax.ShapeDtypeStruct((co, gy // 2, gz_ // 2), BF16),
             jax.ShapeDtypeStruct((ci, planes, gy, gz_), BF16),
-            jax.ShapeDtypeStruct((27 * ci, co), F32),
+            jax.ShapeDtypeStruct((rows, 128), BF16),
         ),
-        in_specs=[vmem] * 3,
-        out_specs=(vmem,) * 3,
+        in_specs=[hbm] * 3,
+        out_specs=(hbm,) * 3,
         scratch_shapes=[
+            pltpu.VMEM((ci, planes, gy, gz_), BF16),
+            pltpu.VMEM((27 * ci, co), BF16),
+            pltpu.VMEM((co, gy // 2, gz_ // 2), BF16),
+            dma((3,)),
+            pltpu.VMEM((co, gy // 2, gz_ // 2), BF16),
+            pltpu.VMEM((ci, planes, gy, gz_), BF16),
+            dma((3,)),
             pltpu.VMEM((ci, gy, gz_), BF16),
             pltpu.VMEM((ci * 2 * gy, gz_), F32),
             pltpu.VMEM((ci * gy, gz_), F32),
@@ -262,18 +299,35 @@
             pltpu.VMEM((3 * co, 1024), BF16),
             pltpu.VMEM((ci * 2 * gy, gz_), F32),
             pltpu.VMEM((rows, 128), F32),
-            pltpu.VMEM((nd - 1, chunk, 128), F32),
+            pltpu.VMEM((group - 1, chunk, 128), F32),
             pltpu.VMEM((chunk, 128), F32),
-            pltpu.VMEM((ns - 1, sub, 128), F32),
-            pltpu.VMEM((chunk, 128), BF16),
+            pltpu.VMEM((line - 1, chunk, 128), F32),
             pltpu.VMEM((rows, 128), BF16),
             dma((2,)), dma((2,)),
-            dma((nd - 1,)), dma((nd - 1,)), dma((ns - 1,)), dma((ns - 1,)),
-            dma((ns - 1,)), dma((ns - 1,)), dma((nd - 1,)), dma((nd - 1,)),
+            dma((group - 1,)), dma((group - 1,)), dma((line - 1,)), dma((line - 1,)),
+            dma((group - 1,)), dma((group - 1,)),
         ],
-        compiler_params=pltpu.CompilerParams(collective_id=0, has_side_effects=True, vmem_limit_bytes=44 * 2**20),
+        compiler_params=pltpu.CompilerParams(collective_id=0, has_side_effects=True, vmem_limit_bytes=60 * 2**20),
         cost_estimate=pl.CostEstimate(flops=400_000_000, bytes_accessed=1_500_000, transcendentals=100_000),
     )(volume[0], k2, cotangent[0, :, 0])
+    act, gv, gk = pl.pallas_call(
+        put,
+        out_shape=(
+            jax.ShapeDtypeStruct(act.shape, BF16),
+            jax.ShapeDtypeStruct(gv.shape, BF16),
+            jax.ShapeDtypeStruct((27 * ci, co), F32),
+        ),
+        in_specs=[hbm] * 3,
+        out_specs=(hbm,) * 3,
+        scratch_shapes=[
+            pltpu.VMEM(act.shape, BF16),
+            pltpu.VMEM(gv.shape, BF16),
+            pltpu.VMEM(packed.shape, BF16),
+            pltpu.VMEM((27 * ci, co), F32),
+            dma((6,)),
+        ],
+        compiler_params=pltpu.CompilerParams(vmem_limit_bytes=60 * 2**20),
+    )(act, gv, packed)
     grad_kernel = gk.reshape(3, 3, 3, ci, co).transpose(4, 3, 0, 1, 2)
     return act[None, :, None], gv[None], grad_kernel
 

time: 31.1 us -> 25.4 us (0.82)
  local copies, waits for them, and re-layouts: 4.9 us -> 0 us
  Pallas kernels: 25.4 us -> 24.7 us
    unnamed x9 -> x0, local copies, waits for them, and re-layouts: 4.9 us -> none
    pallas_call x1, Pallas kernels: 25.4 us -> 22.7 us  [per_device(): pl.pallas_call(functools.partial(kernel, nd, ns, math.sqrt(cells)), out_s...]
    pallas_call x0 -> x1, Pallas kernels: none -> 1.94 us  [per_device(): pl.pallas_call(put, out_shape=(jax.ShapeDtypeStruct(act.shape, BF16), jax...]
where the time goes in v2:
time: 25.4 us; the launch traced here: 25.3 us
  Pallas kernels  24.7 us (97%)
  between operations  0.64 us (3%)
    pallas_call x1, Pallas kernels, per_device(): pl.pallas_call(functools.partial(kernel, nd, ns, math.sqrt(cells)), out_s...  22.7 us
    pallas_call x1, Pallas kernels, per_device(): pl.pallas_call(put, out_shape=(jax.ShapeDtypeStruct(act.shape, BF16), jax...  1.94 us

profile of v2, /device:TPU:0, one launch (start us, length us, event | category | flops | bytes accessed | tf_op | source)
XLA Modules:
  0.0 25.3 jit_solution(2272844270667428919)
XLA Ops:
  0.6 22.7 %shard_map.58 = (bf16[64,8,64]{2,1,0:T(8,128)(2,1)}, bf16[32,2,16,128]{3,2,1,0:T(8,128)(2,1)}, bf16[512,128]{1,0:T(8,128)(2,1)}) custom-call(bf16[32,2,16,128]{3,2,1,0:T(8,128)(2,1)} %bitcast.13, bf16[864,64]{1,0:T(8,128)(2,1)} %bitcast.15, bf16[64,8,64]{2,1,0:T(8,128)(2,1)} %bitcast.16), custom_call_target="tpu_custom_call" | custom-call | flops 400000000 | bytes 1500000 | tf_op jit(solution)/shard_map/pallas_call | solution.py:274
  23.4 1.9 %shard_map.59 = (bf16[64,8,64]{2,1,0:T(8,128)(2,1)}, bf16[32,2,16,128]{3,2,1,0:T(8,128)(2,1)}, f32[864,64]{1,0:T(8,128)}) custom-call(bf16[64,8,64]{2,1,0:T(8,128)(2,1)} %get-tuple-element.9.act, bf16[32,2,16,128]{3,2,1,0:T(8,128)(2,1)} %get-tuple-element.10.gv, bf16[512,128]{1,0:T(8,128)(2,1)} %get-tuple-element.11.packed), custom_call_target="tpu_custom_call" | custom-call | tf_op jit(solution)/shard_map/pallas_call | solution.py:313
